TPU v7x, 1024 devices: a whole 4x8x16 slice. The times are simulated.
1024 devices in a mesh: grp: 32 (over z, core), bal: 32 (over x, y).
Axes of the slice: x: 4, y: 8, z: 16, core: 2. Of those that a mesh axis runs over, the one named last changes fastest.
Arguments:
- tokens: bfloat16 [262144, 1024], P(('grp', 'bal')), may hold values from -6 to 6
- cotangent: bfloat16 [262144, 1024], P(('grp', 'bal')), may hold values from -6 to 6
- w_in: bfloat16 [1024, 2048], replicated, may hold values from -0.1875 to 0.1875
- w_out: bfloat16 [512, 1024], replicated, may hold values from -0.25 to 0.25
- lengths: int32 [32, 32, 2], replicated, may hold values from 64 to 192, as said below
- page_place: int32 [32, 32, 32], replicated, may hold values from 0 to 31, each once within a row
Outputs:
- output: bfloat16 [262144, 1024], P(('grp', 'bal'))
- grad_tokens: bfloat16 [262144, 1024], P(('grp', 'bal'))
- weight_grad: bfloat16 [512, 1024], replicated
Inputs may be any that keep to these rules, and one draw needn't show every extreme that they name: For every g and r, lengths[g, r, 0] + lengths[g, r, 1] = 256; in every group some entry equals 192. For every g and r, page_place[g, r] is a permutation of 0 .. 31.
All inputs are finite; a program needn't handle non-finite values.
Results may differ from a plain program's by a relative error of at most 0.014.
Values may be sent and summed in bfloat16 or wider, within the bound.
A program may use at most 64 MiB of HBM per device.

v0:
```python
import math

import jax
import jax.numpy as jnp
from jax import lax
from jax.sharding import PartitionSpec as P

HEADS = 4


EPS = 1e-05


def layer_norm(values):
    average = jnp.mean(values, axis=-1, keepdims=True)
    centered = values - average
    return centered * lax.rsqrt(jnp.mean(centered * centered, axis=-1, keepdims=True) + EPS)


def branch(tokens_in, w_in, allowed, head_count):
    block_count, block_length, model_width = tokens_in.shape
    inner_width = w_in.shape[1] // 4
    head_size = inner_width // head_count
    normed = layer_norm(tokens_in.astype(jnp.float32)).astype(jnp.bfloat16)
    projected = jnp.dot(
        normed.reshape(block_count * block_length, model_width),
        w_in,
        preferred_element_type=jnp.float32,
    )
    projected = jax.nn.silu(projected).astype(jnp.bfloat16)
    projected = projected.reshape(block_count, block_length, 4, head_count, head_size)
    update = projected[:, :, 0].reshape(block_count, block_length, inner_width)
    value_rows = projected[:, :, 1]
    query_rows = projected[:, :, 2]
    key_rows = projected[:, :, 3]
    scores = jnp.einsum(
        "bihd,bjhd->bhij", query_rows.astype(jnp.float32), key_rows.astype(jnp.float32)
    ) * head_size ** (-0.5)
    weights = jnp.where(allowed[:, None], jax.nn.silu(scores), 0.0).astype(jnp.bfloat16)
    mixed_rows = jnp.einsum(
        "bhij,bjhd->bihd", weights.astype(jnp.float32), value_rows.astype(jnp.float32)
    )
    mixed_rows = mixed_rows.reshape(block_count, block_length, inner_width)
    return (layer_norm(mixed_rows) * update.astype(jnp.float32)).astype(jnp.bfloat16)


def body(tokens, cotangent, w_in, w_out, lengths, page_place):
    peer_count = lax.axis_size("bal")
    group_index = lax.axis_index("grp")
    own_index = lax.axis_index("bal")
    slot_count, model_width = tokens.shape
    page_rows = slot_count // peer_count
    group_lengths = lax.dynamic_index_in_dim(lengths, group_index, 0, keepdims=False)
    own_lengths = lax.dynamic_index_in_dim(group_lengths, own_index, 0, keepdims=False)
    group_place = lax.dynamic_index_in_dim(page_place, group_index, 0, keepdims=False)
    place_row = lax.dynamic_index_in_dim(group_place, own_index, 0, keepdims=False)
    peer_ids = jnp.arange(peer_count, dtype=jnp.int32)
    source_page = jnp.sum(
        jnp.where(place_row[:, None] == peer_ids[None, :], peer_ids[:, None], 0), axis=0
    )
    row_ids = jnp.arange(slot_count, dtype=jnp.int32)
    later_rows = row_ids >= own_lengths[0]
    allowed = (later_rows[:, None] == later_rows[None, :]) & (row_ids[None, :] <= row_ids[:, None])

    def pack_rows(rows_in):
        paged_rows = rows_in.reshape(peer_count, page_rows, rows_in.shape[1])
        return jnp.take(paged_rows, source_page, axis=0).reshape(slot_count, rows_in.shape[1])

    def unpack_rows(rows_in):
        paged_rows = rows_in.reshape(peer_count, page_rows, rows_in.shape[1])
        return jnp.take(paged_rows, place_row, axis=0).reshape(slot_count, rows_in.shape[1])

    def local_branch(tokens_in):
        return branch(tokens_in[None], w_in, allowed[None], HEADS)[0]

    received, received_cot = (
        lax.all_to_all(tokens, "bal", split_axis=0, concat_axis=0, tiled=True),
        lax.all_to_all(cotangent, "bal", split_axis=0, concat_axis=0, tiled=True),
    )
    packed_tokens = pack_rows(received)
    packed_cot = pack_rows(received_cot)
    gated_packed, pull_back = jax.vjp(local_branch, packed_tokens)
    output_packed = packed_tokens.astype(jnp.float32) + jnp.dot(
        gated_packed, w_out, preferred_element_type=jnp.float32
    )
    grad_gated = lax.dot_general(
        packed_cot, w_out, (((1,), (1,)), ((), ())), preferred_element_type=jnp.float32
    ).astype(jnp.bfloat16)
    branch_packed = pull_back(grad_gated)[0]
    grad_packed = (packed_cot.astype(jnp.float32) + branch_packed.astype(jnp.float32)).astype(
        jnp.bfloat16
    )
    partial_grad = lax.dot_general(
        gated_packed, packed_cot, (((0,), (0,)), ((), ())), preferred_element_type=jnp.float32
    )
    output, grad_tokens = (
        lax.all_to_all(
            unpack_rows(output_packed.astype(jnp.bfloat16)),
            "bal",
            split_axis=0,
            concat_axis=0,
            tiled=True,
        ),
        lax.all_to_all(unpack_rows(grad_packed), "bal", split_axis=0, concat_axis=0, tiled=True),
    )
    grad_scale = 1.0 / math.sqrt(lax.axis_size("grp") * peer_count * slot_count)
    total_grad = lax.psum(partial_grad, ("grp", "bal"))
    weight_grad = (total_grad * grad_scale).astype(jnp.bfloat16)
    return (output, grad_tokens, weight_grad)


def solution(mesh):
    placed = (P(("grp", "bal"), None), P(("grp", "bal"), None), P(), P(), P(), P())
    return jax.shard_map(
        body,
        mesh=mesh,
        in_specs=placed,
        out_specs=(P(("grp", "bal"), None), P(("grp", "bal"), None), P()),
        check_vma=False,
    )
```

profile of v0, /device:TPU:1, one launch (start us, length us, event | category | flops | bytes accessed | tf_op | source)
XLA Modules:
  0.0 620.5 jit_solution(3033583586039871980)
XLA Ops:
  7.2 10.6 %all-to-all-start = ((bf16[32,8,1024]{2,1,0:T(8,128)(2,1)}), bf16[32,8,1024]{2,1,0:T(8,128)(2,1)S(1)}, u32[]{:S(2)}, u32[]{:S(2)}) async-start(bf16[32,8,1024]{2,1,0:T(8,128)(2,1)} %bitcast.158), calls=%async_computation | async-start | bytes 1048576 | tf_op jit(solution)/shard_map/all_to_all | solution.py:77
  20.7 8.5 %all-to-all-done = bf16[32,8,1024]{2,1,0:T(8,128)(2,1)S(1)} async-done(((bf16[32,8,1024]{2,1,0:T(8,128)(2,1)}), bf16[32,8,1024]{2,1,0:T(8,128)(2,1)S(1)}, u32[]{:S(2)}, u32[]{:S(2)}) %all-to-all-start) | async-done | bytes 524320 | tf_op jit(solution)/shard_map/all_to_all | solution.py:77
  29.2 5.6 all-to-all-start.2
  36.1 5.3 multiply_convert_fusion.1
  41.4 1.8 reshape.468
  44.5 2.6 select_convert_fusion
  49.3 1.6 gather_fusion.2
  51.0 1.7 multiply_reduce_fusion
  53.8 1.8 copy.49
  55.6 2.1 fusion.18
  57.7 2.1 fusion.25
  66.8 2.9 copy.51
  69.7 5.1 fusion.22
  76.6 1.6 gather_fusion.3
  78.3 2.4 gather_fusion.1
  80.7 2.2 broadcast_select_fusion
  82.8 9.3 %all-to-all-start.1 = ((bf16[32,8,1024]{2,1,0:T(8,128)(2,1)}), bf16[32,8,1024]{2,1,0:T(8,128)(2,1)}, u32[]{:S(2)}, u32[]{:S(2)}) async-start(bf16[32,8,1024]{2,1,0:T(8,128)(2,1)} %get-tuple-element.16), calls=%async_computation.1 | async-start | bytes 1048576 | tf_op jit(solution)/shard_map/all_to_all | solution.py:97
  92.4 1.8 fusion.36
  94.3 9.2 %all-to-all-done.1 = bf16[32,8,1024]{2,1,0:T(8,128)(2,1)} async-done(((bf16[32,8,1024]{2,1,0:T(8,128)(2,1)}), bf16[32,8,1024]{2,1,0:T(8,128)(2,1)}, u32[]{:S(2)}, u32[]{:S(2)}) %all-to-all-start.1) | async-done | bytes 524320 | tf_op jit(solution)/shard_map/all_to_all | solution.py:97
  103.5 5.5 all-to-all-start.3
  109.0 11.7 %all-to-all-done.3 = bf16[32,8,1024]{2,1,0:T(8,128)(2,1)S(1)} async-done(((bf16[32,8,1024]{2,1,0:T(8,128)(2,1)}), bf16[32,8,1024]{2,1,0:T(8,128)(2,1)S(1)}, u32[]{:S(2)}, u32[]{:S(2)}) %all-to-all-start.3) | async-done | bytes 524320 | tf_op jit(solution)/shard_map/all_to_all | solution.py:104
  120.7 487.4 %all-reduce.6.cloned.1.call-done = f32[512,1024]{1,0:T(8,128)} async-done(((f32[512,1024]{1,0:T(8,128)}), f32[512,1024]{1,0:T(8,128)}) %all-reduce.6.cloned.1.call-update) | async-done | bytes 2097168 | tf_op jit(solution)/shard_map/psum | solution.py:107
  608.1 2.8 multiply_convert_fusion
  611.0 1.9 copy.78
  (55 shorter events, 18.7 us)
Async XLA Ops:
  7.2 43.8 %copy-start = (bf16[512,1024]{1,0:T(8,128)(2,1)S(1)}, bf16[512,1024]{1,0:T(8,128)(2,1)}, u32[]{:S(2)}) copy-start(bf16[512,1024]{1,0:T(8,128)(2,1)} %param.11) | copy-start | bytes 3145732
  7.2 22.0 %all-to-all-start = ((bf16[32,8,1024]{2,1,0:T(8,128)(2,1)}), bf16[32,8,1024]{2,1,0:T(8,128)(2,1)S(1)}, u32[]{:S(2)}, u32[]{:S(2)}) async-start(bf16[32,8,1024]{2,1,0:T(8,128)(2,1)} %bitcast.158), calls=%async_computation | async-start | bytes 1048576 | tf_op jit(solution)/shard_map/all_to_all | solution.py:77
  29.2 20.1 %all-to-all-start.2 = ((bf16[32,8,1024]{2,1,0:T(8,128)(2,1)}), bf16[32,8,1024]{2,1,0:T(8,128)(2,1)}, u32[]{:S(2)}, u32[]{:S(2)}) async-start(bf16[32,8,1024]{2,1,0:T(8,128)(2,1)} %bitcast.159), calls=%async_computation.2 | async-start | bytes 1048576 | tf_op jit(solution)/shard_map/all_to_all | solution.py:78
  44.5 2.6 copy-start.6
  47.1 0.8 copy-start.3
  51.0 1.7 copy-start.1
  57.7 2.1 copy-start.5
  57.7 3.1 copy-start.4
  59.8 2.0 copy-start.2
  82.8 20.6 %all-to-all-start.1 = ((bf16[32,8,1024]{2,1,0:T(8,128)(2,1)}), bf16[32,8,1024]{2,1,0:T(8,128)(2,1)}, u32[]{:S(2)}, u32[]{:S(2)}) async-start(bf16[32,8,1024]{2,1,0:T(8,128)(2,1)} %get-tuple-element.16), calls=%async_computation.1 | async-start | bytes 1048576 | tf_op jit(solution)/shard_map/all_to_all | solution.py:97
  92.1 516.0 %all-reduce.6.cloned.1.call-start = ((), (), s32[]{:S(2)}) async-start(), calls=%async_computation.4 | async-start | bytes 4194304 | tf_op jit(solution)/shard_map/psum | solution.py:107
  103.5 17.2 %all-to-all-start.3 = ((bf16[32,8,1024]{2,1,0:T(8,128)(2,1)}), bf16[32,8,1024]{2,1,0:T(8,128)(2,1)S(1)}, u32[]{:S(2)}, u32[]{:S(2)}) async-start(bf16[32,8,1024]{2,1,0:T(8,128)(2,1)} %get-tuple-element.15), calls=%async_computation.3 | async-start | bytes 1048576 | tf_op jit(solution)/shard_map/all_to_all | solution.py:104
Sparse Core Ops, SparseCore 0:
  98.3 509.7 all-reduce.5
where the time goes:
time: 622 us; the launch traced here: 620 us
  waiting for transfers between devices  517 us (83%)
  starting transfers between devices  31 us (5%)
  matrix products  24.3 us (4%)
  local copies, waits for them, and re-layouts  19.8 us (3%)
  between operations  14.3 us (2%)
  other arithmetic  14.2 us (2%)
    psum x1, waiting for transfers between devices, body(): total_grad = lax.psum(partial_grad, ('grp', 'bal'))  487 us
  transfers between devices with their start and end apart: 5, of which 4 were waited for; matrix products, arithmetic and copies ran while one was open for 3% of the time, Pallas kernels for 0%

commit v1 on v0

v1 whole, which is shorter than its diff:
```python
import functools
import math

import jax
import jax.numpy as jnp
from jax import lax
from jax.experimental import pallas as pl
from jax.experimental.pallas import tpu as pltpu
from jax.sharding import PartitionSpec as P

HEADS = 4
EPS = 1e-05
MESH = pl.DeviceIdType.MESH
F32 = jnp.float32
BF16 = jnp.bfloat16

NX, NY, NZ, NC = 4, 8, 16, 2
NB = NX * NY
PAGE = 8
ROWS = NB * PAGE
D = 1024
E = 512
HS = E // HEADS
TOK, GG, GATED, GRAD, RA, RX, RY, RZ, GZ, GY, GX, GC = range(12)


def nt(a, b):
    return lax.dot_general(a, b, (((1,), (1,)), ((), ())), preferred_element_type=F32)


def tn(a, b):
    return lax.dot_general(a, b, (((0,), (0,)), ((), ())), preferred_element_type=F32)


def nn(a, b):
    return jnp.dot(a, b, preferred_element_type=F32)


def sigmoid(v):
    return 0.5 * jnp.tanh(0.5 * v) + 0.5


def row_mean(v):
    return jnp.mean(v, axis=-1, keepdims=True)


def kernel(
    scale_out,
    tok3_hbm, tok_hbm, cot_hbm, w_in_hbm, w_out_hbm, len_hbm, place_hbm,
    out_hbm, grad_hbm, wg_hbm,
    cot, tok, w_in, w_out, lens, place,
    tokr, gg_s, ggr, gated_s, gatedr, grad_s, gradr,
    zin, inv1, normed, proj, dsilu, mask, wts, fac, mixed, inv2, dm, dpre, dn,
    gown, p_send, p_own, r_a, a_send, r_x, b_send, r_y, c_send, r_z, gz, wg,
    out_v, grad_v,
    ssem, rsem, lsem,
):
    grp = lax.axis_index("grp")
    me = lax.axis_index("bal")
    z, core = grp // NC, lax.rem(grp, NC)
    x, y = me // NY, lax.rem(me, NY)

    loads = [
        pltpu.make_async_copy(src, dst, lsem.at[i])
        for i, (src, dst) in enumerate(
            (
                (cot_hbm, cot),
                (w_out_hbm, w_out),
                (w_in_hbm, w_in),
                (tok_hbm, tok),
                (len_hbm.at[grp], lens),
                (place_hbm.at[grp], place),
            )
        )
    ]
    for load in loads:
        load.start()

    def bal_peer(k):
        dy = lax.rem(3 * k, NY)
        dx = lax.rem(k + k // NY, NX)
        return lax.rem(x + dx, NX) * NY + lax.rem(y + dy, NY)

    def z_peer(d):
        return lax.rem(z + d, NZ) * NC + core

    barrier = pltpu.get_barrier_semaphore()

    @pl.loop(1, NB)
    def _(k):
        pl.semaphore_signal(barrier, inc=1, device_id={"bal": bal_peer(k)}, device_id_type=MESH)

    @pl.loop(1, NZ)
    def _(d):
        pl.semaphore_signal(barrier, inc=1, device_id={"grp": z_peer(d)}, device_id_type=MESH)

    partner = z * NC + 1 - core
    pl.semaphore_signal(barrier, inc=1, device_id={"grp": partner}, device_id_type=MESH)
    pl.semaphore_wait(barrier, NB - 1 + NZ - 1 + 1)

    def spread(src, dst, i):
        @pl.loop(1, NB)
        def _(k):
            peer = bal_peer(k)
            pltpu.make_async_remote_copy(
                src_ref=src.at[peer], dst_ref=dst.at[me],
                send_sem=ssem.at[i], recv_sem=rsem.at[i],
                device_id={"bal": peer}, device_id_type=MESH,
            ).start()

        pltpu.make_async_copy(src.at[me], dst.at[me], rsem.at[i]).start()

    def remote(src, dst, i, device):
        pltpu.make_async_remote_copy(
            src_ref=src, dst_ref=dst, send_sem=ssem.at[i], recv_sem=rsem.at[i],
            device_id=device, device_id_type=MESH,
        ).start()

    def wait_recv(ref, i):
        pltpu.make_async_copy(ref, ref, rsem.at[i]).wait()

    def wait_send(ref, i):
        pltpu.make_async_copy(ref, ref, ssem.at[i]).wait()

    spread(tok3_hbm, tokr, TOK)

    loads[0].wait()
    loads[1].wait()
    gg_s[...] = nt(cot[...], w_out[...]).reshape(NB, PAGE, E).astype(BF16)
    spread(gg_s, ggr, GG)

    loads[4].wait()
    loads[5].wait()
    lane2 = lax.broadcasted_iota(jnp.int32, (2, NB), 1)
    row2 = lax.broadcasted_iota(jnp.int32, (2, NB), 0)
    first = jnp.sum(
        jnp.where((lane2 == me) & (row2 == 0), lens[...], 0).astype(F32), axis=(0, 1), keepdims=True
    )
    sub = lax.broadcasted_iota(jnp.int32, (NB, NB), 0)
    place_row = jnp.sum(
        jnp.where(sub == me, place[...], 0).astype(F32), axis=0, keepdims=True
    )
    r_id = lax.broadcasted_iota(jnp.int32, (ROWS, NB), 0)
    p_id = lax.broadcasted_iota(jnp.int32, (ROWS, NB), 1)
    picked = jnp.where((r_id // PAGE) == p_id, jnp.broadcast_to(place_row, (ROWS, NB)), 0.0)
    page_col = jnp.sum(picked, axis=1, keepdims=True)
    in_page = lax.rem(lax.broadcasted_iota(jnp.int32, (ROWS, 1), 0), PAGE).astype(F32)
    pos_col = page_col * PAGE + in_page
    e_p = lax.broadcasted_iota(jnp.int32, (NB, ROWS), 0)
    e_r = lax.broadcasted_iota(jnp.int32, (NB, ROWS), 1)
    spread_pages = jnp.where((e_r // PAGE) == e_p, 1.0, 0.0).astype(BF16)
    page_row = nn(jnp.broadcast_to(place_row, (PAGE, NB)).astype(BF16), spread_pages)[0:1]
    in_page_row = lax.rem(lax.broadcasted_iota(jnp.int32, (1, ROWS), 1), PAGE).astype(F32)
    pos_row = page_row * PAGE + in_page_row
    start_col = jnp.where(pos_col >= first, jnp.broadcast_to(first, (ROWS, 1)), 0.0)
    mask[...] = jnp.where((pos_row <= pos_col) & (pos_row >= start_col), 1.0, 0.0)

    loads[2].wait()
    wait_recv(tokr, TOK)

    @pl.loop(0, ROWS // 32)
    def _(i):
        rows = pl.ds(pl.multiple_of(i * 32, 32), 32)
        v = tokr[pl.ds(i * 4, 4)].astype(F32).reshape(32, D)
        c = v - row_mean(v)
        inv = lax.rsqrt(row_mean(c * c) + EPS)
        n = c * inv
        zin[rows, :] = n
        inv1[rows, :] = jnp.broadcast_to(inv, (32, 128))
        normed[rows, :] = n.astype(BF16)

    @pl.loop(0, 4 * E // 256)
    def _(j):
        cols = pl.ds(pl.multiple_of(j * 256, 256), 256)
        pre = nn(normed[...], w_in[:, cols])
        sig = sigmoid(pre)
        proj[:, cols] = (pre * sig).astype(BF16)
        dsilu[:, cols] = sig * (1.0 + pre * (1.0 - sig))

    def head_cols(block, h):
        return pl.ds(pl.multiple_of(block * E + h * HS, HS), HS)

    @pl.loop(0, HEADS)
    def _(h):
        s = nt(proj[:, head_cols(2, h)], proj[:, head_cols(3, h)]) * (HS ** -0.5)
        sig = sigmoid(s)
        allowed = mask[...]
        w = (s * sig * allowed).astype(BF16)
        wts[h] = w
        fac[h] = allowed * (HS ** -0.5) * sig * (1.0 + s * (1.0 - sig))
        mixed[:, head_cols(0, h)] = nn(w, proj[:, head_cols(1, h)])

    @pl.loop(0, ROWS // 32)
    def _(i):
        rows = pl.ds(pl.multiple_of(i * 32, 32), 32)
        v = mixed[rows, :]
        c = v - row_mean(v)
        inv = lax.rsqrt(row_mean(c * c) + EPS)
        n = c * inv
        mixed[rows, :] = n
        inv2[rows, :] = jnp.broadcast_to(inv, (32, 128))
        g = n * proj[rows, 0:E].astype(F32)
        gated_s[pl.ds(i * 4, 4)] = g.reshape(4, PAGE, E).astype(BF16)

    spread(gated_s, gatedr, GATED)

    wait_recv(ggr, GG)

    @pl.loop(0, ROWS // 32)
    def _(i):
        rows = pl.ds(pl.multiple_of(i * 32, 32), 32)
        g = ggr[pl.ds(i * 4, 4)].astype(F32).reshape(32, E)
        n = mixed[rows, :]
        du = (g * n).astype(BF16).astype(F32)
        dpre[rows, 0:E] = (du * dsilu[rows, 0:E]).astype(BF16)
        dz = g * proj[rows, 0:E].astype(F32)
        back = inv2[rows, 0:1] * (dz - row_mean(dz) - n * row_mean(dz * n))
        dm[rows, :] = back.astype(BF16)

    @pl.loop(0, HEADS)
    def _(h):
        dmh = dm[:, head_cols(0, h)]
        vc, qc, kc = head_cols(1, h), head_cols(2, h), head_cols(3, h)
        dv = tn(wts[h], dmh).astype(BF16).astype(F32)
        dpre[:, vc] = (dv * dsilu[:, vc]).astype(BF16)
        dw = nt(dmh, proj[:, vc]).astype(BF16).astype(F32)
        ds = (dw * fac[h]).astype(BF16)
        dq = nn(ds, proj[:, kc]).astype(BF16).astype(F32)
        dpre[:, qc] = (dq * dsilu[:, qc]).astype(BF16)
        dk = tn(ds, proj[:, qc]).astype(BF16).astype(F32)
        dpre[:, kc] = (dk * dsilu[:, kc]).astype(BF16)

    @pl.loop(0, D // 256)
    def _(j):
        cols = pl.ds(pl.multiple_of(j * 256, 256), 256)
        dn[:, cols] = nt(dpre[...], w_in[cols, :]).astype(BF16)

    @pl.loop(0, ROWS // 32)
    def _(i):
        rows = pl.ds(pl.multiple_of(i * 32, 32), 32)
        d = dn[rows, :].astype(F32)
        n = zin[rows, :]
        back = inv1[rows, 0:1] * (d - row_mean(d) - n * row_mean(d * n))
        grad_s[pl.ds(i * 4, 4)] = back.reshape(4, PAGE, D).astype(BF16)

    spread(grad_s, gradr, GRAD)

    wait_recv(gatedr, GATED)

    @pl.loop(0, ROWS // 32)
    def _(i):
        rows = pl.ds(pl.multiple_of(i * 32, 32), 32)
        gown[rows, :] = gatedr[pl.ds(i * 4, 4)].astype(F32).reshape(32, E).astype(BF16)

    half = E // NC
    nh = half // PAGE
    other_cols = pl.ds(pl.multiple_of((1 - core) * half, half), half)
    own_cols = pl.ds(pl.multiple_of(core * half, half), half)
    p_send[...] = tn(gown[:, other_cols], cot[...]).reshape(nh, PAGE, D).astype(BF16)
    remote(p_send, r_a, RA, {"grp": partner})
    p_own[...] = tn(gown[:, own_cols], cot[...]).reshape(nh, PAGE, D)

    loads[3].wait()

    @pl.loop(0, D // 256)
    def _(j):
        cols = pl.ds(pl.multiple_of(j * 256, 256), 256)
        out_v[:, cols] = (tok[:, cols].astype(F32) + nn(gown[...], w_out[:, cols])).astype(BF16)

    out_copy = pltpu.make_async_copy(out_v, out_hbm, lsem.at[0])
    out_copy.start()

    wait_recv(r_a, RA)

    @pl.loop(0, nh // 4)
    def _(i):
        blocks = pl.ds(i * 4, 4)
        a = p_own[blocks] + r_a[blocks].astype(F32)
        p_own[blocks] = a
        a_send[blocks] = a.astype(BF16)

    for d in range(1, NX):
        px = lax.rem(x + d, NX)
        remote(
            a_send.at[pl.ds(px * NY, NY)], r_x.at[pl.ds((d - 1) * NY, NY)], RX, {"bal": px * NY + y}
        )
    wait_recv(r_x, RX)

    @pl.loop(0, NY)
    def _(i):
        b = p_own[x * NY + i]
        for d in range(NX - 1):
            b = b + r_x[d * NY + i].astype(F32)
        p_own[x * NY + i] = b
        b_send[i] = b.astype(BF16)

    for d in range(1, NY):
        py = lax.rem(y + d, NY)
        remote(b_send.at[py], r_y.at[d - 1], RY, {"bal": x * NY + py})
    wait_recv(r_y, RY)
    total = p_own[me]
    for d in range(NY - 1):
        total = total + r_y[d].astype(F32)
    for p in range(8):
        c_send[p] = total[:, p * 128 : (p + 1) * 128]
    zp = lax.rem(z, 8)
    r_z[z] = c_send[zp]

    @pl.loop(1, NZ)
    def _(d):
        pz = lax.rem(z + d, NZ)
        remote(c_send.at[lax.rem(pz, 8)], r_z.at[z], RZ, {"grp": pz * NC + core})

    wait_recv(r_z.at[pl.ds(0, NZ - 1)], RZ)
    piece = r_z[0]
    for p in range(1, NZ):
        piece = piece + r_z[p]
    gz[zp] = (piece * scale_out).astype(BF16)

    for d in (1, -1, 2, -2, 3, -3, 4):
        remote(gz.at[zp], gz.at[zp], GZ, {"grp": z_peer(d + NZ)})
    wait_recv(gz.at[pl.ds(0, 7)], GZ)
    block = core * nh + me
    for p in range(8):
        wg[block, :, p * 128 : (p + 1) * 128] = gz[p]
    for d in range(1, NY):
        py = lax.rem(y + d, NY)
        remote(wg.at[block], wg.at[block], GY, {"bal": x * NY + py})
    wait_recv(wg.at[pl.ds(0, NY - 1)], GY)
    xs = pl.ds(core * nh + x * NY, NY)
    for d in range(1, NX):
        px = lax.rem(x + d, NX)
        remote(wg.at[xs], wg.at[xs], GX, {"bal": px * NY + y})
    wait_recv(wg.at[pl.ds(0, (NX - 1) * NY)], GX)
    cs = pl.ds(core * nh, nh)
    remote(wg.at[cs], wg.at[cs], GC, {"grp": partner})

    wait_recv(gradr, GRAD)

    @pl.loop(0, ROWS // 32)
    def _(i):
        rows = pl.ds(pl.multiple_of(i * 32, 32), 32)
        b = gradr[pl.ds(i * 4, 4)].astype(F32).reshape(32, D)
        grad_v[rows, :] = (cot[rows, :].astype(F32) + b).astype(BF16)

    grad_copy = pltpu.make_async_copy(grad_v, grad_hbm, lsem.at[1])
    grad_copy.start()
    wait_recv(wg.at[pl.ds(0, nh)], GC)
    wg_copy = pltpu.make_async_copy(wg, wg_hbm, lsem.at[2])
    wg_copy.start()

    for ref, i in ((tok3_hbm, TOK), (gg_s, GG), (gated_s, GATED), (grad_s, GRAD)):
        wait_send(ref.at[pl.ds(0, NB - 1)], i)
    wait_send(p_send, RA)
    wait_send(a_send.at[pl.ds(0, (NX - 1) * NY)], RX)
    wait_send(b_send.at[pl.ds(0, NY - 1)], RY)
    wait_send(r_z.at[pl.ds(0, NZ - 1)], RZ)
    wait_send(gz.at[pl.ds(0, 7)], GZ)
    wait_send(wg.at[pl.ds(0, NY - 1)], GY)
    wait_send(wg.at[pl.ds(0, (NX - 1) * NY)], GX)
    wait_send(wg.at[pl.ds(0, nh)], GC)
    out_copy.wait()
    grad_copy.wait()
    wg_copy.wait()


def body(tokens, cotangent, w_in, w_out, lengths, page_place):
    nblk = E // PAGE
    nh = nblk // NC
    scale_out = 1.0 / math.sqrt(NZ * NC * NB * ROWS)
    vm = pltpu.VMEM
    scratch = [
        vm((ROWS, D), BF16), vm((ROWS, D), BF16), vm((D, 4 * E), BF16), vm((E, D), BF16),
        vm((2, NB), jnp.int32), vm((NB, NB), jnp.int32),
        vm((NB, PAGE, D), BF16),
        vm((NB, PAGE, E), BF16), vm((NB, PAGE, E), BF16),
        vm((NB, PAGE, E), BF16), vm((NB, PAGE, E), BF16),
        vm((NB, PAGE, D), BF16), vm((NB, PAGE, D), BF16),
        vm((ROWS, D), F32), vm((ROWS, 128), F32), vm((ROWS, D), BF16),
        vm((ROWS, 4 * E), BF16), vm((ROWS, 4 * E), F32), vm((ROWS, ROWS), F32),
        vm((HEADS, ROWS, ROWS), BF16), vm((HEADS, ROWS, ROWS), F32),
        vm((ROWS, E), F32), vm((ROWS, 128), F32), vm((ROWS, E), BF16),
        vm((ROWS, 4 * E), BF16), vm((ROWS, D), BF16),
        vm((ROWS, E), BF16),
        vm((nh, PAGE, D), BF16), vm((nh, PAGE, D), F32), vm((nh, PAGE, D), BF16),
        vm((nh, PAGE, D), BF16), vm(((NX - 1) * NY, PAGE, D), BF16),
        vm((NY, PAGE, D), BF16), vm((NY - 1, PAGE, D), BF16),
        vm((8, PAGE, 128), F32), vm((NZ, PAGE, 128), F32), vm((8, PAGE, 128), BF16),
        vm((nblk, PAGE, D), BF16),
        vm((ROWS, D), BF16), vm((ROWS, D), BF16),
        pltpu.SemaphoreType.DMA((12,)), pltpu.SemaphoreType.DMA((12,)), pltpu.SemaphoreType.DMA((6,)),
    ]
    hbm = pl.BlockSpec(memory_space=pltpu.HBM)
    output, grad_tokens, weight_grad = pl.pallas_call(
        functools.partial(kernel, scale_out),
        out_shape=(
            jax.ShapeDtypeStruct((ROWS, D), BF16),
            jax.ShapeDtypeStruct((ROWS, D), BF16),
            jax.ShapeDtypeStruct((nblk, PAGE, D), BF16),
        ),
        in_specs=[hbm] * 7,
        out_specs=(hbm, hbm, hbm),
        scratch_shapes=scratch,
        compiler_params=pltpu.CompilerParams(
            collective_id=0, has_side_effects=True, vmem_limit_bytes=60 * 1024 * 1024
        ),
    )(
        tokens.reshape(NB, PAGE, D), tokens, cotangent, w_in, w_out,
        jnp.swapaxes(lengths, 1, 2), page_place,
    )
    return output, grad_tokens, weight_grad.reshape(E, D)


def solution(mesh):
    placed = (P(("grp", "bal"), None), P(("grp", "bal"), None), P(), P(), P(), P())
    return jax.shard_map(
        body,
        mesh=mesh,
        in_specs=placed,
        out_specs=(P(("grp", "bal"), None), P(("grp", "bal"), None), P()),
        check_vma=False,
    )
```

time: 622 us -> 111 us (0.18)
  waiting for transfers between devices: 517 us -> 0 us
  Pallas kernels: 0 us -> 104 us
  starting transfers between devices: 31 us -> 0 us
  matrix products: 24.3 us -> 0 us
  other arithmetic: 14.2 us -> 0 us
  local copies, waits for them, and re-layouts: 19.8 us -> 6 us
  between operations: 14.3 us -> 0.64 us
    psum x1 -> x0, waiting for transfers between devices: 487 us -> none  [body(): total_grad = lax.psum(partial_grad, ('grp', 'bal'))]
    pallas_call x0 -> x1, Pallas kernels: none -> 104 us  [body(): pl.pallas_call(functools.partial(kernel, scale_out), out_shape=(jax.Shape...]
    all_to_all x4 -> x0, starting transfers between devices: 31 us -> none  [the longest x1 10.6 us: body(): lax.all_to_all(tokens, 'bal', split_axis=0, concat_axis=0, tiled=True)]
    all_to_all x4 -> x0, waiting for transfers between devices: 29.5 us -> none  [the longest x1 11.7 us: body(): lax.all_to_all(unpack_rows(grad_packed), 'bal', split_axis=0, concat_axis...]
    dot_general x11 -> x0, matrix products: 24.3 us -> none  [the longest x2 10.4 us: branch(): jnp.dot(normed.reshape(block_count * block_length, model_width), w_in, pr...]
    gather x4 -> x0, local copies, waits for them, and re-layouts: 6.24 us -> none  [the longest x2 4.03 us: unpack_rows(): jnp.take(paged_rows, place_row, axis=0)]
  transfers between devices with their start and end apart: 5 -> 0, of which waited for: 4 -> 0; matrix products, arithmetic and copies ran while one was open for 3% -> 0% of each run, Pallas kernels for 0% -> 0%
where the time goes in v1:
time: 111 us; the launch traced here: 110 us
  Pallas kernels  104 us (94%)
  local copies, waits for them, and re-layouts  6 us (5%)
    pallas_call x1, Pallas kernels, body(): pl.pallas_call(functools.partial(kernel, scale_out), out_shape=(jax.Shape...  104 us
    unnamed x3, local copies, waits for them, and re-layouts  6 us

profile of v1, /device:TPU:1, one launch (start us, length us, event | category | flops | bytes accessed | tf_op | source)
XLA Modules:
  0.0 110.3 jit_solution(18116368668948078790)
XLA Ops:
  0.6 103.6 %shard_map.85 = (bf16[256,1024]{1,0:T(8,128)(2,1)}, bf16[256,1024]{1,0:T(8,128)(2,1)}, bf16[64,8,1024]{2,1,0:T(8,128)(2,1)}) custom-call(bf16[32,8,1024]{2,1,0:T(8,128)(2,1)} %bitcast.3, bf16[256,1024]{1,0:T(8,128)(2,1)} %tok_hbm.1, bf16[256,1024]{1,0:T(8,128)(2,1)} %cot_hbm.1, bf16[1024,2048]{1,0:T(8,128)(2,1)} %w_in_hbm.1, bf16[512,1024]{1,0:T(8,128)(2,1)} %w_out_hbm.1, ...), custom_call_target="tpu_custom_call" | custom-call | tf_op jit(solution)/shard_map/pallas_call | solution.py:394
  104.3 1.9 %copy.12 = bf16[256,1024]{1,0:T(8,128)(2,1)} copy(bf16[256,1024]{1,0:T(8,128)(2,1)} %get-tuple-element.12) | data formatting | bytes 1048576
  106.2 1.9 %copy.13 = bf16[256,1024]{1,0:T(8,128)(2,1)} copy(bf16[256,1024]{1,0:T(8,128)(2,1)} %get-tuple-element.13) | data formatting | bytes 1048576
  108.0 2.3 %copy.14 = bf16[512,1024]{1,0:T(8,128)(2,1)} copy(bf16[512,1024]{1,0:T(8,128)(2,1)} %bitcast.4) | data formatting | bytes 2097152

commit v2 on v1

--- a/solution.py
+++ b/solution.py
@@ -16,12 +16,18 @@
 
 NX, NY, NZ, NC = 4, 8, 16, 2
 NB = NX * NY
+ZL = 4
+ZH = max(NZ // ZL, 1)
 PAGE = 8
 ROWS = NB * PAGE
 D = 1024
 E = 512
 HS = E // HEADS
-TOK, GG, GATED, GRAD, RA, RX, RY, RZ, GZ, GY, GX, GC = range(12)
+TOK, GG, GATED, GRAD = range(4)
+HALVES = 2
+RA, RX, RY, RZ, RV, GZ, GY, GX, GC = range(4, 4 + 9 * HALVES, HALVES)
+HD = D // HALVES
+NP = HD // 128
 
 
 def nt(a, b):
@@ -51,7 +57,7 @@
     cot, tok, w_in, w_out, lens, place,
     tokr, gg_s, ggr, gated_s, gatedr, grad_s, gradr,
     zin, inv1, normed, proj, dsilu, mask, wts, fac, mixed, inv2, dm, dpre, dn,
-    gown, p_send, p_own, r_a, a_send, r_x, b_send, r_y, c_send, r_z, gz, wg,
+    gown, p_send, p_own, r_a, a_send, r_x, b_send, r_y, c_send, r_z, r_v, gz, wg,
     out_v, grad_v,
     ssem, rsem, lsem,
 ):
@@ -59,6 +65,7 @@
     me = lax.axis_index("bal")
     z, core = grp // NC, lax.rem(grp, NC)
     x, y = me // NY, lax.rem(me, NY)
+    zh, zl = z // ZL, lax.rem(z, ZL)
 
     loads = [
         pltpu.make_async_copy(src, dst, lsem.at[i])
@@ -81,8 +88,11 @@
         dx = lax.rem(k + k // NY, NX)
         return lax.rem(x + dx, NX) * NY + lax.rem(y + dy, NY)
 
-    def z_peer(d):
-        return lax.rem(z + d, NZ) * NC + core
+    def run_peer(d):
+        return (zh * ZL + lax.rem(zl + d, ZL)) * NC + core
+
+    def cross_peer(d):
+        return (lax.rem(zh + d, ZH) * ZL + zl) * NC + core
 
     barrier = pltpu.get_barrier_semaphore()
 
@@ -90,16 +100,15 @@
     def _(k):
         pl.semaphore_signal(barrier, inc=1, device_id={"bal": bal_peer(k)}, device_id_type=MESH)
 
-    @pl.loop(1, NZ)
-    def _(d):
-        pl.semaphore_signal(barrier, inc=1, device_id={"grp": z_peer(d)}, device_id_type=MESH)
-
+    z_peers = [run_peer(d) for d in range(1, ZL)] + [cross_peer(d) for d in range(1, ZH)] if NZ > 1 else []
+    for peer in z_peers:
+        pl.semaphore_signal(barrier, inc=1, device_id={"grp": peer}, device_id_type=MESH)
     partner = z * NC + 1 - core
     pl.semaphore_signal(barrier, inc=1, device_id={"grp": partner}, device_id_type=MESH)
-    pl.semaphore_wait(barrier, NB - 1 + NZ - 1 + 1)
-
-    def spread(src, dst, i):
-        @pl.loop(1, NB)
+    pl.semaphore_wait(barrier, NB - 1 + len(z_peers) + 1)
+
+    def spread(src, dst, i, low=1, high=NB):
+        @pl.loop(low, high)
         def _(k):
             peer = bal_peer(k)
             pltpu.make_async_remote_copy(
@@ -108,7 +117,8 @@
                 device_id={"bal": peer}, device_id_type=MESH,
             ).start()
 
-        pltpu.make_async_copy(src.at[me], dst.at[me], rsem.at[i]).start()
+        if high == NB:
+            pltpu.make_async_copy(src.at[me], dst.at[me], rsem.at[i]).start()
 
     def remote(src, dst, i, device):
         pltpu.make_async_remote_copy(
@@ -158,9 +168,8 @@
     loads[2].wait()
     wait_recv(tokr, TOK)
 
-    @pl.loop(0, ROWS // 32)
-    def _(i):
-        rows = pl.ds(pl.multiple_of(i * 32, 32), 32)
+    for i in range(ROWS // 32):
+        rows = pl.ds(i * 32, 32)
         v = tokr[pl.ds(i * 4, 4)].astype(F32).reshape(32, D)
         c = v - row_mean(v)
         inv = lax.rsqrt(row_mean(c * c) + EPS)
@@ -169,19 +178,17 @@
         inv1[rows, :] = jnp.broadcast_to(inv, (32, 128))
         normed[rows, :] = n.astype(BF16)
 
-    @pl.loop(0, 4 * E // 256)
-    def _(j):
-        cols = pl.ds(pl.multiple_of(j * 256, 256), 256)
+    for j in range(4 * E // 256):
+        cols = pl.ds(j * 256, 256)
         pre = nn(normed[...], w_in[:, cols])
         sig = sigmoid(pre)
         proj[:, cols] = (pre * sig).astype(BF16)
         dsilu[:, cols] = sig * (1.0 + pre * (1.0 - sig))
 
     def head_cols(block, h):
-        return pl.ds(pl.multiple_of(block * E + h * HS, HS), HS)
-
-    @pl.loop(0, HEADS)
-    def _(h):
+        return pl.ds(block * E + h * HS, HS)
+
+    for h in range(HEADS):
         s = nt(proj[:, head_cols(2, h)], proj[:, head_cols(3, h)]) * (HS ** -0.5)
         sig = sigmoid(s)
         allowed = mask[...]
@@ -190,9 +197,8 @@
         fac[h] = allowed * (HS ** -0.5) * sig * (1.0 + s * (1.0 - sig))
         mixed[:, head_cols(0, h)] = nn(w, proj[:, head_cols(1, h)])
 
-    @pl.loop(0, ROWS // 32)
-    def _(i):
-        rows = pl.ds(pl.multiple_of(i * 32, 32), 32)
+    for i in range(ROWS // 32):
+        rows = pl.ds(i * 32, 32)
         v = mixed[rows, :]
         c = v - row_mean(v)
         inv = lax.rsqrt(row_mean(c * c) + EPS)
@@ -206,9 +212,8 @@
 
     wait_recv(ggr, GG)
 
-    @pl.loop(0, ROWS // 32)
-    def _(i):
-        rows = pl.ds(pl.multiple_of(i * 32, 32), 32)
+    for i in range(ROWS // 32):
+        rows = pl.ds(i * 32, 32)
         g = ggr[pl.ds(i * 4, 4)].astype(F32).reshape(32, E)
         n = mixed[rows, :]
         du = (g * n).astype(BF16).astype(F32)
@@ -217,8 +222,7 @@
         back = inv2[rows, 0:1] * (dz - row_mean(dz) - n * row_mean(dz * n))
         dm[rows, :] = back.astype(BF16)
 
-    @pl.loop(0, HEADS)
-    def _(h):
+    for h in range(HEADS):
         dmh = dm[:, head_cols(0, h)]
         vc, qc, kc = head_cols(1, h), head_cols(2, h), head_cols(3, h)
         dv = tn(wts[h], dmh).astype(BF16).astype(F32)
@@ -230,14 +234,12 @@
         dk = tn(ds, proj[:, qc]).astype(BF16).astype(F32)
         dpre[:, kc] = (dk * dsilu[:, kc]).astype(BF16)
 
-    @pl.loop(0, D // 256)
-    def _(j):
-        cols = pl.ds(pl.multiple_of(j * 256, 256), 256)
+    for j in range(D // 256):
+        cols = pl.ds(j * 256, 256)
         dn[:, cols] = nt(dpre[...], w_in[cols, :]).astype(BF16)
 
-    @pl.loop(0, ROWS // 32)
-    def _(i):
-        rows = pl.ds(pl.multiple_of(i * 32, 32), 32)
+    for i in range(ROWS // 32):
+        rows = pl.ds(i * 32, 32)
         d = dn[rows, :].astype(F32)
         n = zin[rows, :]
         back = inv1[rows, 0:1] * (d - row_mean(d) - n * row_mean(d * n))
@@ -247,121 +249,163 @@
 
     wait_recv(gatedr, GATED)
 
-    @pl.loop(0, ROWS // 32)
-    def _(i):
-        rows = pl.ds(pl.multiple_of(i * 32, 32), 32)
+    for i in range(ROWS // 32):
+        rows = pl.ds(i * 32, 32)
         gown[rows, :] = gatedr[pl.ds(i * 4, 4)].astype(F32).reshape(32, E).astype(BF16)
 
     half = E // NC
     nh = half // PAGE
     other_cols = pl.ds(pl.multiple_of((1 - core) * half, half), half)
     own_cols = pl.ds(pl.multiple_of(core * half, half), half)
-    p_send[...] = tn(gown[:, other_cols], cot[...]).reshape(nh, PAGE, D).astype(BF16)
-    remote(p_send, r_a, RA, {"grp": partner})
-    p_own[...] = tn(gown[:, own_cols], cot[...]).reshape(nh, PAGE, D)
+
+    def term(cols, h):
+        return tn(gown[:, cols], cot[:, h * HD : (h + 1) * HD]).reshape(nh, PAGE, HD)
+
+    for h in range(HALVES):
+        p_send[h] = term(other_cols, h).astype(BF16)
+        remote(p_send.at[h], r_a.at[h], RA + h, {"grp": partner})
+    for h in range(HALVES):
+        p_own[h] = term(own_cols, h)
+
+    for h in range(HALVES):
+        wait_recv(r_a.at[h], RA + h)
+        for i in range(0, nh, 4):
+            a = p_own[h, i : i + 4] + r_a[h, i : i + 4].astype(F32)
+            p_own[h, i : i + 4] = a
+            a_send[h, i : i + 4] = a.astype(BF16)
+        for d in (1, 3, 2):
+            px = lax.rem(x + d, NX)
+            remote(
+                a_send.at[h, pl.ds(px * NY, NY)], r_x.at[h, pl.ds((d - 1) * NY, NY)],
+                RX + h, {"bal": px * NY + y},
+            )
 
     loads[3].wait()
-
-    @pl.loop(0, D // 256)
-    def _(j):
-        cols = pl.ds(pl.multiple_of(j * 256, 256), 256)
+    for j in range(D // 256):
+        cols = pl.ds(j * 256, 256)
         out_v[:, cols] = (tok[:, cols].astype(F32) + nn(gown[...], w_out[:, cols])).astype(BF16)
-
     out_copy = pltpu.make_async_copy(out_v, out_hbm, lsem.at[0])
     out_copy.start()
 
-    wait_recv(r_a, RA)
-
-    @pl.loop(0, nh // 4)
-    def _(i):
-        blocks = pl.ds(i * 4, 4)
-        a = p_own[blocks] + r_a[blocks].astype(F32)
-        p_own[blocks] = a
-        a_send[blocks] = a.astype(BF16)
-
-    for d in range(1, NX):
-        px = lax.rem(x + d, NX)
-        remote(
-            a_send.at[pl.ds(px * NY, NY)], r_x.at[pl.ds((d - 1) * NY, NY)], RX, {"bal": px * NY + y}
-        )
-    wait_recv(r_x, RX)
-
-    @pl.loop(0, NY)
-    def _(i):
-        b = p_own[x * NY + i]
+    for h in range(HALVES):
+        wait_recv(r_x.at[h], RX + h)
+        b = p_own[h, pl.ds(x * NY, NY)]
         for d in range(NX - 1):
-            b = b + r_x[d * NY + i].astype(F32)
-        p_own[x * NY + i] = b
-        b_send[i] = b.astype(BF16)
-
-    for d in range(1, NY):
-        py = lax.rem(y + d, NY)
-        remote(b_send.at[py], r_y.at[d - 1], RY, {"bal": x * NY + py})
-    wait_recv(r_y, RY)
-    total = p_own[me]
-    for d in range(NY - 1):
-        total = total + r_y[d].astype(F32)
-    for p in range(8):
-        c_send[p] = total[:, p * 128 : (p + 1) * 128]
-    zp = lax.rem(z, 8)
-    r_z[z] = c_send[zp]
-
-    @pl.loop(1, NZ)
-    def _(d):
-        pz = lax.rem(z + d, NZ)
-        remote(c_send.at[lax.rem(pz, 8)], r_z.at[z], RZ, {"grp": pz * NC + core})
-
-    wait_recv(r_z.at[pl.ds(0, NZ - 1)], RZ)
-    piece = r_z[0]
-    for p in range(1, NZ):
-        piece = piece + r_z[p]
-    gz[zp] = (piece * scale_out).astype(BF16)
-
-    for d in (1, -1, 2, -2, 3, -3, 4):
-        remote(gz.at[zp], gz.at[zp], GZ, {"grp": z_peer(d + NZ)})
-    wait_recv(gz.at[pl.ds(0, 7)], GZ)
+            b = b + r_x[h, d * NY : (d + 1) * NY].astype(F32)
+        p_own[h, pl.ds(x * NY, NY)] = b
+        b_send[h] = b.astype(BF16)
+        for d in range(1, NY):
+            py = lax.rem(y + d, NY)
+            remote(b_send.at[h, py], r_y.at[h, d - 1], RY + h, {"bal": x * NY + py})
+
+    for h in range(HALVES):
+        wait_recv(r_y.at[h], RY + h)
+        total = p_own[h, me]
+        for d in range(NY - 1):
+            total = total + r_y[h, d].astype(F32)
+        for p in range(NP):
+            c_send[h, p] = total[:, p * 128 : (p + 1) * 128]
+        r_z[h, zl] = c_send[h, zl]
+        if NZ > 1:
+            for d in range(1, ZL):
+                remote(c_send.at[h, lax.rem(zl + d, ZL)], r_z.at[h, zl], RZ + h, {"grp": run_peer(d)})
+
+    for h in range(HALVES):
+        piece = r_z[h, 0] if NZ == 1 else None
+        if NZ > 1:
+            wait_recv(r_z.at[h, pl.ds(0, ZL - 1)], RZ + h)
+            piece = r_z[h, 0] + r_z[h, 1] + r_z[h, 2] + r_z[h, 3]
+        r_v[h, zh] = piece
+        for d in range(1, ZH):
+            remote(r_v.at[h, zh], r_v.at[h, zh], RV + h, {"grp": cross_peer(d)})
+
+    for h in range(HALVES):
+        if NZ > 1:
+            wait_recv(r_v.at[h, pl.ds(0, ZH - 1)], RV + h)
+        piece = r_v[h, 0]
+        for p in range(1, ZH):
+            piece = piece + r_v[h, p]
+        gz[h, zl] = (piece * scale_out).astype(BF16)
+        if NZ > 1:
+            for d in range(1, ZL):
+                remote(gz.at[h, zl], gz.at[h, zl], GZ + h, {"grp": run_peer(d)})
+
     block = core * nh + me
-    for p in range(8):
-        wg[block, :, p * 128 : (p + 1) * 128] = gz[p]
-    for d in range(1, NY):
-        py = lax.rem(y + d, NY)
-        remote(wg.at[block], wg.at[block], GY, {"bal": x * NY + py})
-    wait_recv(wg.at[pl.ds(0, NY - 1)], GY)
+    for h in range(HALVES):
+        if NZ > 1:
+            wait_recv(gz.at[h, pl.ds(0, ZL - 1)], GZ + h)
+        for p in range(NP):
+            wg[h, block, :, p * 128 : (p + 1) * 128] = gz[h, p]
+        for d in range(1, NY):
+            py = lax.rem(y + d, NY)
+            remote(wg.at[h, block], wg.at[h, block], GY + h, {"bal": x * NY + py})
+
     xs = pl.ds(core * nh + x * NY, NY)
-    for d in range(1, NX):
-        px = lax.rem(x + d, NX)
-        remote(wg.at[xs], wg.at[xs], GX, {"bal": px * NY + y})
-    wait_recv(wg.at[pl.ds(0, (NX - 1) * NY)], GX)
+    for h in range(HALVES):
+        wait_recv(wg.at[h, pl.ds(0, NY - 1)], GY + h)
+        for d in (1, 3, 2):
+            px = lax.rem(x + d, NX)
+            remote(wg.at[h, xs], wg.at[h, xs], GX + h, {"bal": px * NY + y})
+
     cs = pl.ds(core * nh, nh)
-    remote(wg.at[cs], wg.at[cs], GC, {"grp": partner})
+    for h in range(HALVES):
+        wait_recv(wg.at[h, pl.ds(0, (NX - 1) * NY)], GX + h)
+        remote(wg.at[h, cs], wg.at[h, cs], GC + h, {"grp": partner})
 
     wait_recv(gradr, GRAD)
-
-    @pl.loop(0, ROWS // 32)
-    def _(i):
-        rows = pl.ds(pl.multiple_of(i * 32, 32), 32)
+    for i in range(ROWS // 32):
+        rows = pl.ds(i * 32, 32)
         b = gradr[pl.ds(i * 4, 4)].astype(F32).reshape(32, D)
         grad_v[rows, :] = (cot[rows, :].astype(F32) + b).astype(BF16)
-
     grad_copy = pltpu.make_async_copy(grad_v, grad_hbm, lsem.at[1])
     grad_copy.start()
-    wait_recv(wg.at[pl.ds(0, nh)], GC)
-    wg_copy = pltpu.make_async_copy(wg, wg_hbm, lsem.at[2])
-    wg_copy.start()
+
+    wg_copies = []
+    for h in range(HALVES):
+        wait_recv(wg.at[h, pl.ds(0, nh)], GC + h)
+        wg_copies.append(
+            pltpu.make_async_copy(wg.at[h], wg_hbm.at[:, :, pl.ds(h * HD, HD)], lsem.at[2 + h])
+        )
+        wg_copies[h].start()
 
     for ref, i in ((tok3_hbm, TOK), (gg_s, GG), (gated_s, GATED), (grad_s, GRAD)):
         wait_send(ref.at[pl.ds(0, NB - 1)], i)
-    wait_send(p_send, RA)
-    wait_send(a_send.at[pl.ds(0, (NX - 1) * NY)], RX)
-    wait_send(b_send.at[pl.ds(0, NY - 1)], RY)
-    wait_send(r_z.at[pl.ds(0, NZ - 1)], RZ)
-    wait_send(gz.at[pl.ds(0, 7)], GZ)
-    wait_send(wg.at[pl.ds(0, NY - 1)], GY)
-    wait_send(wg.at[pl.ds(0, (NX - 1) * NY)], GX)
-    wait_send(wg.at[pl.ds(0, nh)], GC)
-    out_copy.wait()
-    grad_copy.wait()
-    wg_copy.wait()
+    for h in range(HALVES):
+        wait_send(p_send.at[h], RA + h)
+        wait_send(r_x.at[h], RX + h)
+        wait_send(r_y.at[h], RY + h)
+        if NZ > 1:
+            wait_send(r_z.at[h, pl.ds(0, ZL - 1)], RZ + h)
+            wait_send(r_v.at[h, pl.ds(0, ZH - 1)], RV + h)
+            wait_send(gz.at[h, pl.ds(0, ZL - 1)], GZ + h)
+        wait_send(wg.at[h, pl.ds(0, NY - 1)], GY + h)
+        wait_send(wg.at[h, pl.ds(0, (NX - 1) * NY)], GX + h)
+        wait_send(wg.at[h, pl.ds(0, nh)], GC + h)
+    for copy in (out_copy, grad_copy, *wg_copies):
+        copy.wait()
+
+
+def copy_kernel(n, *refs):
+    sources, targets, held, sems = refs[:n], refs[n : 2 * n], refs[2 * n : 3 * n], refs[3 * n]
+    parts = []
+    for i in range(n):
+        step = sources[i].shape[0] // 2
+        for j in range(2):
+            part = pl.ds(j * step, step)
+            loads, stores = sems.at[0, 2 * i + j], sems.at[1, 2 * i + j]
+            parts.append(
+                (
+                    pltpu.make_async_copy(sources[i].at[part], held[i].at[part], loads),
+                    pltpu.make_async_copy(held[i].at[part], targets[i].at[part], stores),
+                )
+            )
+    for load, _ in parts:
+        load.start()
+    for load, store in parts:
+        load.wait()
+        store.start()
+    for _, store in parts:
+        store.wait()
 
 
 def body(tokens, cotangent, w_in, w_out, lengths, page_place):
@@ -382,16 +426,20 @@
         vm((ROWS, E), F32), vm((ROWS, 128), F32), vm((ROWS, E), BF16),
         vm((ROWS, 4 * E), BF16), vm((ROWS, D), BF16),
         vm((ROWS, E), BF16),
-        vm((nh, PAGE, D), BF16), vm((nh, PAGE, D), F32), vm((nh, PAGE, D), BF16),
-        vm((nh, PAGE, D), BF16), vm(((NX - 1) * NY, PAGE, D), BF16),
-        vm((NY, PAGE, D), BF16), vm((NY - 1, PAGE, D), BF16),
-        vm((8, PAGE, 128), F32), vm((NZ, PAGE, 128), F32), vm((8, PAGE, 128), BF16),
-        vm((nblk, PAGE, D), BF16),
+        vm((HALVES, nh, PAGE, HD), BF16), vm((HALVES, nh, PAGE, HD), F32),
+        vm((HALVES, nh, PAGE, HD), BF16), vm((HALVES, nh, PAGE, HD), BF16),
+        vm((HALVES, (NX - 1) * NY, PAGE, HD), BF16),
+        vm((HALVES, NY, PAGE, HD), BF16), vm((HALVES, NY - 1, PAGE, HD), BF16),
+        vm((HALVES, NP, PAGE, 128), F32), vm((HALVES, ZL, PAGE, 128), F32),
+        vm((HALVES, ZH, PAGE, 128), F32),
+        vm((HALVES, NP, PAGE, 128), BF16),
+        vm((HALVES, nblk, PAGE, HD), BF16),
         vm((ROWS, D), BF16), vm((ROWS, D), BF16),
-        pltpu.SemaphoreType.DMA((12,)), pltpu.SemaphoreType.DMA((12,)), pltpu.SemaphoreType.DMA((6,)),
+        pltpu.SemaphoreType.DMA((4 + 9 * HALVES,)), pltpu.SemaphoreType.DMA((4 + 9 * HALVES,)),
+        pltpu.SemaphoreType.DMA((8,)),
     ]
     hbm = pl.BlockSpec(memory_space=pltpu.HBM)
-    output, grad_tokens, weight_grad = pl.pallas_call(
+    results = pl.pallas_call(
         functools.partial(kernel, scale_out),
         out_shape=(
             jax.ShapeDtypeStruct((ROWS, D), BF16),
@@ -408,6 +456,15 @@
         tokens.reshape(NB, PAGE, D), tokens, cotangent, w_in, w_out,
         jnp.swapaxes(lengths, 1, 2), page_place,
     )
+    output, grad_tokens, weight_grad = pl.pallas_call(
+        functools.partial(copy_kernel, len(results)),
+        out_shape=tuple(jax.ShapeDtypeStruct(r.shape, r.dtype) for r in results),
+        in_specs=[hbm] * len(results),
+        out_specs=(hbm,) * len(results),
+        scratch_shapes=[pltpu.VMEM(r.shape, r.dtype) for r in results]
+        + [pltpu.SemaphoreType.DMA((2, 2 * len(results)))],
+        compiler_params=pltpu.CompilerParams(vmem_limit_bytes=60 * 1024 * 1024),
+    )(*results)
     return output, grad_tokens, weight_grad.reshape(E, D)
 
 

time: 111 us -> 97.9 us (0.88)
  Pallas kernels: 104 us -> 97.1 us
  local copies, waits for them, and re-layouts: 6 us -> 0 us
    pallas_call x1, Pallas kernels: 104 us -> 94.7 us  [body(): pl.pallas_call(functools.partial(kernel, scale_out), out_shape=(jax.Shape...]
    unnamed x3 -> x0, local copies, waits for them, and re-layouts: 6 us -> none
    pallas_call x0 -> x1, Pallas kernels: none -> 2.43 us  [body(): pl.pallas_call(functools.partial(copy_kernel, len(results)), out_shape=tu...]
where the time goes in v2:
time: 97.9 us; the launch traced here: 97.8 us
  Pallas kernels  97.1 us (99%)
    pallas_call x1, Pallas kernels, body(): pl.pallas_call(functools.partial(kernel, scale_out), out_shape=(jax.Shape...  94.7 us
    pallas_call x1, Pallas kernels, body(): pl.pallas_call(functools.partial(copy_kernel, len(results)), out_shape=tu...  2.43 us

profile of v2, /device:TPU:1, one launch (start us, length us, event | category | flops | bytes accessed | tf_op | source)
XLA Modules:
  0.0 97.8 jit_solution(3807500002370041021)
XLA Ops:
  0.6 94.7 %shard_map.85 = (bf16[256,1024]{1,0:T(8,128)(2,1)}, bf16[256,1024]{1,0:T(8,128)(2,1)}, bf16[64,8,1024]{2,1,0:T(8,128)(2,1)}) custom-call(bf16[32,8,1024]{2,1,0:T(8,128)(2,1)} %bitcast.3, bf16[256,1024]{1,0:T(8,128)(2,1)} %tok_hbm.1, bf16[256,1024]{1,0:T(8,128)(2,1)} %cot_hbm.1, bf16[1024,2048]{1,0:T(8,128)(2,1)} %w_in_hbm.1, bf16[512,1024]{1,0:T(8,128)(2,1)} %w_out_hbm.1, ...), custom_call_target="tpu_custom_call" | custom-call | tf_op jit(solution)/shard_map/pallas_call | solution.py:442
  95.3 2.4 %shard_map.86 = (bf16[256,1024]{1,0:T(8,128)(2,1)}, bf16[256,1024]{1,0:T(8,128)(2,1)}, bf16[64,8,1024]{2,1,0:T(8,128)(2,1)}) custom-call(bf16[256,1024]{1,0:T(8,128)(2,1)} %get-tuple-element.9.refs_0_, bf16[256,1024]{1,0:T(8,128)(2,1)} %get-tuple-element.10.refs_1_, bf16[64,8,1024]{2,1,0:T(8,128)(2,1)} %get-tuple-element.11.refs_2_), custom_call_target="tpu_custom_call" | custom-call | tf_op jit(solution)/shard_map/pallas_call | solution.py:459

commit v3 on v2

--- a/solution.py
+++ b/solution.py
@@ -245,8 +245,6 @@
         back = inv1[rows, 0:1] * (d - row_mean(d) - n * row_mean(d * n))
         grad_s[pl.ds(i * 4, 4)] = back.reshape(4, PAGE, D).astype(BF16)
 
-    spread(grad_s, gradr, GRAD)
-
     wait_recv(gatedr, GATED)
 
     for i in range(ROWS // 32):
@@ -273,7 +271,7 @@
             a = p_own[h, i : i + 4] + r_a[h, i : i + 4].astype(F32)
             p_own[h, i : i + 4] = a
             a_send[h, i : i + 4] = a.astype(BF16)
-        for d in (1, 3, 2):
+        for d in (2, 1, 3):
             px = lax.rem(x + d, NX)
             remote(
                 a_send.at[h, pl.ds(px * NY, NY)], r_x.at[h, pl.ds((d - 1) * NY, NY)],
@@ -294,9 +292,11 @@
             b = b + r_x[h, d * NY : (d + 1) * NY].astype(F32)
         p_own[h, pl.ds(x * NY, NY)] = b
         b_send[h] = b.astype(BF16)
-        for d in range(1, NY):
+        for d in (4, 3, 5, 2, 6, 1, 7):
             py = lax.rem(y + d, NY)
             remote(b_send.at[h, py], r_y.at[h, d - 1], RY + h, {"bal": x * NY + py})
+
+    spread(grad_s, gradr, GRAD)
 
     for h in range(HALVES):
         wait_recv(r_y.at[h], RY + h)
@@ -316,7 +316,7 @@
             wait_recv(r_z.at[h, pl.ds(0, ZL - 1)], RZ + h)
             piece = r_z[h, 0] + r_z[h, 1] + r_z[h, 2] + r_z[h, 3]
         r_v[h, zh] = piece
-        for d in range(1, ZH):
+        for d in sorted(range(1, ZH), key=lambda d: -min(d, ZH - d)):
             remote(r_v.at[h, zh], r_v.at[h, zh], RV + h, {"grp": cross_peer(d)})
 
     for h in range(HALVES):
@@ -336,14 +336,14 @@
             wait_recv(gz.at[h, pl.ds(0, ZL - 1)], GZ + h)
         for p in range(NP):
             wg[h, block, :, p * 128 : (p + 1) * 128] = gz[h, p]
-        for d in range(1, NY):
+        for d in (4, 3, 5, 2, 6, 1, 7):
             py = lax.rem(y + d, NY)
             remote(wg.at[h, block], wg.at[h, block], GY + h, {"bal": x * NY + py})
 
     xs = pl.ds(core * nh + x * NY, NY)
     for h in range(HALVES):
         wait_recv(wg.at[h, pl.ds(0, NY - 1)], GY + h)
-        for d in (1, 3, 2):
+        for d in (2, 1, 3):
             px = lax.rem(x + d, NX)
             remote(wg.at[h, xs], wg.at[h, xs], GX + h, {"bal": px * NY + y})
 

time: 97.9 us -> 94.6 us (0.966)
  Pallas kernels: 97.1 us -> 93.8 us
    pallas_call x1, Pallas kernels: 94.7 us -> 91.4 us  [body(): pl.pallas_call(functools.partial(kernel, scale_out), out_shape=(jax.Shape...]
where the time goes in v3:
time: 94.6 us; the launch traced here: 94.5 us
  Pallas kernels  93.8 us (99%)
    pallas_call x1, Pallas kernels, body(): pl.pallas_call(functools.partial(kernel, scale_out), out_shape=(jax.Shape...  91.4 us
    pallas_call x1, Pallas kernels, body(): pl.pallas_call(functools.partial(copy_kernel, len(results)), out_shape=tu...  2.43 us

profile of v3, /device:TPU:1, one launch (start us, length us, event | category | flops | bytes accessed | tf_op | source)
XLA Modules:
  0.0 94.5 jit_solution(3317791447098178994)
XLA Ops:
  0.6 91.4 %shard_map.85 = (bf16[256,1024]{1,0:T(8,128)(2,1)}, bf16[256,1024]{1,0:T(8,128)(2,1)}, bf16[64,8,1024]{2,1,0:T(8,128)(2,1)}) custom-call(bf16[32,8,1024]{2,1,0:T(8,128)(2,1)} %bitcast.3, bf16[256,1024]{1,0:T(8,128)(2,1)} %tok_hbm.1, bf16[256,1024]{1,0:T(8,128)(2,1)} %cot_hbm.1, bf16[1024,2048]{1,0:T(8,128)(2,1)} %w_in_hbm.1, bf16[512,1024]{1,0:T(8,128)(2,1)} %w_out_hbm.1, ...), custom_call_target="tpu_custom_call" | custom-call | tf_op jit(solution)/shard_map/pallas_call | solution.py:442
  92.0 2.4 %shard_map.86 = (bf16[256,1024]{1,0:T(8,128)(2,1)}, bf16[256,1024]{1,0:T(8,128)(2,1)}, bf16[64,8,1024]{2,1,0:T(8,128)(2,1)}) custom-call(bf16[256,1024]{1,0:T(8,128)(2,1)} %get-tuple-element.9.refs_0_, bf16[256,1024]{1,0:T(8,128)(2,1)} %get-tuple-element.10.refs_1_, bf16[64,8,1024]{2,1,0:T(8,128)(2,1)} %get-tuple-element.11.refs_2_), custom_call_target="tpu_custom_call" | custom-call | tf_op jit(solution)/shard_map/pallas_call | solution.py:459

commit v4 on v3

--- a/solution.py
+++ b/solution.py
@@ -210,6 +210,39 @@
 
     spread(gated_s, gatedr, GATED)
 
+    wait_recv(gatedr, GATED)
+
+    for i in range(ROWS // 32):
+        rows = pl.ds(i * 32, 32)
+        gown[rows, :] = gatedr[pl.ds(i * 4, 4)].astype(F32).reshape(32, E).astype(BF16)
+
+    half = E // NC
+    nh = half // PAGE
+    other_cols = pl.ds(pl.multiple_of((1 - core) * half, half), half)
+    own_cols = pl.ds(pl.multiple_of(core * half, half), half)
+
+    def term(cols, h):
+        return tn(gown[:, cols], cot[:, h * HD : (h + 1) * HD]).reshape(nh, PAGE, HD)
+
+    for h in range(HALVES):
+        p_send[h] = term(other_cols, h).astype(BF16)
+        remote(p_send.at[h], r_a.at[h], RA + h, {"grp": partner})
+    for h in range(HALVES):
+        p_own[h] = term(own_cols, h)
+
+    for h in range(HALVES):
+        wait_recv(r_a.at[h], RA + h)
+        for i in range(0, nh, 4):
+            a = p_own[h, i : i + 4] + r_a[h, i : i + 4].astype(F32)
+            p_own[h, i : i + 4] = a
+            a_send[h, i : i + 4] = a.astype(BF16)
+        for d in (2, 1, 3):
+            px = lax.rem(x + d, NX)
+            remote(
+                a_send.at[h, pl.ds(px * NY, NY)], r_x.at[h, pl.ds((d - 1) * NY, NY)],
+                RX + h, {"bal": px * NY + y},
+            )
+
     wait_recv(ggr, GG)
 
     for i in range(ROWS // 32):
@@ -244,39 +277,6 @@
         n = zin[rows, :]
         back = inv1[rows, 0:1] * (d - row_mean(d) - n * row_mean(d * n))
         grad_s[pl.ds(i * 4, 4)] = back.reshape(4, PAGE, D).astype(BF16)
-
-    wait_recv(gatedr, GATED)
-
-    for i in range(ROWS // 32):
-        rows = pl.ds(i * 32, 32)
-        gown[rows, :] = gatedr[pl.ds(i * 4, 4)].astype(F32).reshape(32, E).astype(BF16)
-
-    half = E // NC
-    nh = half // PAGE
-    other_cols = pl.ds(pl.multiple_of((1 - core) * half, half), half)
-    own_cols = pl.ds(pl.multiple_of(core * half, half), half)
-
-    def term(cols, h):
-        return tn(gown[:, cols], cot[:, h * HD : (h + 1) * HD]).reshape(nh, PAGE, HD)
-
-    for h in range(HALVES):
-        p_send[h] = term(other_cols, h).astype(BF16)
-        remote(p_send.at[h], r_a.at[h], RA + h, {"grp": partner})
-    for h in range(HALVES):
-        p_own[h] = term(own_cols, h)
-
-    for h in range(HALVES):
-        wait_recv(r_a.at[h], RA + h)
-        for i in range(0, nh, 4):
-            a = p_own[h, i : i + 4] + r_a[h, i : i + 4].astype(F32)
-            p_own[h, i : i + 4] = a
-            a_send[h, i : i + 4] = a.astype(BF16)
-        for d in (2, 1, 3):
-            px = lax.rem(x + d, NX)
-            remote(
-                a_send.at[h, pl.ds(px * NY, NY)], r_x.at[h, pl.ds((d - 1) * NY, NY)],
-                RX + h, {"bal": px * NY + y},
-            )
 
     loads[3].wait()
     for j in range(D // 256):

time: 94.6 us -> 94.7 us (level)
  no operation moved by 1% of the time
where the time goes in v4:
time: 94.7 us; the launch traced here: 94.5 us
  Pallas kernels  93.9 us (99%)
    pallas_call x1, Pallas kernels, body(): pl.pallas_call(functools.partial(kernel, scale_out), out_shape=(jax.Shape...  91.4 us
    pallas_call x1, Pallas kernels, body(): pl.pallas_call(functools.partial(copy_kernel, len(results)), out_shape=tu...  2.43 us

profile of v4, /device:TPU:1, one launch (start us, length us, event | category | flops | bytes accessed | tf_op | source)
XLA Modules:
  0.0 94.5 jit_solution(11444062862890556623)
XLA Ops:
  0.6 91.4 %shard_map.85 = (bf16[256,1024]{1,0:T(8,128)(2,1)}, bf16[256,1024]{1,0:T(8,128)(2,1)}, bf16[64,8,1024]{2,1,0:T(8,128)(2,1)}) custom-call(bf16[32,8,1024]{2,1,0:T(8,128)(2,1)} %bitcast.3, bf16[256,1024]{1,0:T(8,128)(2,1)} %tok_hbm.1, bf16[256,1024]{1,0:T(8,128)(2,1)} %cot_hbm.1, bf16[1024,2048]{1,0:T(8,128)(2,1)} %w_in_hbm.1, bf16[512,1024]{1,0:T(8,128)(2,1)} %w_out_hbm.1, ...), custom_call_target="tpu_custom_call" | custom-call | tf_op jit(solution)/shard_map/pallas_call | solution.py:442
  92.1 2.4 %shard_map.86 = (bf16[256,1024]{1,0:T(8,128)(2,1)}, bf16[256,1024]{1,0:T(8,128)(2,1)}, bf16[64,8,1024]{2,1,0:T(8,128)(2,1)}) custom-call(bf16[256,1024]{1,0:T(8,128)(2,1)} %get-tuple-element.9.refs_0_, bf16[256,1024]{1,0:T(8,128)(2,1)} %get-tuple-element.10.refs_1_, bf16[64,8,1024]{2,1,0:T(8,128)(2,1)} %get-tuple-element.11.refs_2_), custom_call_target="tpu_custom_call" | custom-call | tf_op jit(solution)/shard_map/pallas_call | solution.py:459
